TPU v7x, 512 devices: a whole 4x8x8 slice. The times are simulated.
512 devices in a mesh: ct: 128 (over y, z, core), bl: 4 (over x).
Axes of the slice: x: 4, y: 8, z: 8, core: 2. Of those that a mesh axis runs over, the one named last changes fastest.
Arguments:
- samples: bfloat16 [1024, 65536], P('ct', 'bl'), may hold values from -6 to 6
- history: bfloat16 [1024, 1536], P('ct'), may hold values from -6 to 6
- tile_cell: int32 [256, 36], P('ct'), may hold values from 0 to 7
- tile_weight: float32 [256, 36], P('ct'), may hold values from 0.25 to 4
Outputs:
- grid: float32 [8, 256, 2, 128, 128], P('bl', 'ct')
All inputs are finite; a program needn't handle non-finite values.
Results may differ from a plain program's by a relative error of at most 0.0048.
Values may be sent and summed in bfloat16 or wider, within the bound.
A program may use at most 64 MiB of HBM per device.

v0:
```python
import math
import jax
import jax.numpy as jnp
from jax import lax
from jax.sharding import PartitionSpec as P

CH = 256
BLOCK = 128
TAPS = 4
SPECTRA = 128
CELL_DEV = 2
FRAME = 512


def from_behind(value, axis, by):
    size = lax.axis_size(axis)
    pairs = [(i, i + by) for i in range(size) if 0 <= i + by < size]
    return lax.ppermute(value, axis, pairs)


def filter_table():
    span = TAPS * FRAME
    sample_pos = jnp.arange(span, dtype=jnp.float32) + 0.5
    window = jnp.sinc(sample_pos / FRAME - TAPS / 2.0) * (
        0.5 - 0.5 * jnp.cos(2.0 * math.pi * sample_pos / span)
    )
    phase_int = (
        jnp.arange(FRAME, dtype=jnp.int32)[:, None]
        * jnp.arange(CH, dtype=jnp.int32)[None, :]
        % FRAME
    )
    angle = phase_int.astype(jnp.float32) * (2.0 * math.pi / FRAME)
    basis = jnp.concatenate([jnp.cos(angle), -jnp.sin(angle)], axis=1)
    table = window.reshape(TAPS, FRAME)[:, :, None] * basis[None] * (2.0 / math.sqrt(FRAME))
    return table.astype(jnp.bfloat16)


def cell_selector(tile_cell, weights, tri_index, is_valid, cell_count):
    picked = jnp.take(tile_cell, tri_index, axis=1)
    picked_weight = jnp.take(weights, tri_index, axis=1) * is_valid
    cell_ids = lax.broadcasted_iota(jnp.int32, (cell_count, 1, 1), 0)
    return (picked[None] == cell_ids).astype(jnp.float32) * picked_weight[None]


def shards(samples, history, tile_cell, tile_weight):
    bl_size = lax.axis_size("bl")
    bl_index = lax.axis_index("bl")
    inputs_dev = samples.shape[0]
    spec_dev = samples.shape[1] // FRAME
    table = filter_table()
    frames = samples.reshape(inputs_dev, spec_dev, FRAME)
    last_frames = frames[:, spec_dev - (TAPS - 1) :, :]
    earlier = from_behind(last_frames, "bl", 1)
    earlier = jnp.where(bl_index == 0, history.reshape(inputs_dev, TAPS - 1, FRAME), earlier)
    extended = jnp.concatenate([earlier, frames], axis=1)
    accum = jnp.zeros((2 * CH, inputs_dev, spec_dev), jnp.float32)
    for tap_index in range(TAPS):
        accum = accum + jnp.einsum(
            "psn,nk->kps",
            extended[:, tap_index : tap_index + spec_dev],
            table[tap_index],
            preferred_element_type=jnp.float32,
        )
    spectra = accum.astype(jnp.bfloat16).reshape(2, CH, inputs_dev, spec_dev)
    turned = lax.all_to_all(spectra, "ct", split_axis=1, concat_axis=2, tiled=True)
    channels = turned.shape[1]
    inputs = turned.shape[2]
    blocks = inputs // BLOCK
    cell_count = CELL_DEV * bl_size
    weights = tile_weight * (1.0 / math.sqrt(SPECTRA))
    rows_each = blocks // bl_size
    shard_part = lax.all_gather(turned, "bl", axis=3, tiled=True)
    row_part = lax.dynamic_slice_in_dim(
        shard_part, bl_index * rows_each * BLOCK, rows_each * BLOCK, 2
    )
    products = jnp.einsum(
        "acps,bcqs->cabpq", row_part, shard_part, preferred_element_type=jnp.float32
    )
    visibility = jnp.stack(
        [products[:, 0, 0] + products[:, 1, 1], products[:, 1, 0] - products[:, 0, 1]], axis=1
    )
    visibility = visibility.reshape(channels, 2, rows_each, BLOCK, blocks, BLOCK)
    row_index = bl_index * rows_each + jnp.arange(rows_each, dtype=jnp.int32)
    col_index = jnp.arange(blocks, dtype=jnp.int32)
    is_valid = col_index[None, :] >= row_index[:, None]
    tri_index = (
        row_index[:, None] * blocks
        - row_index[:, None] * (row_index[:, None] - 1) // 2
        + col_index[None, :]
        - row_index[:, None]
    )
    tri_index = jnp.where(is_valid, tri_index, 0).reshape(-1)
    selector = cell_selector(
        tile_cell, weights, tri_index, is_valid.reshape(-1).astype(jnp.float32), cell_count
    )
    selector = selector.reshape(cell_count, channels, rows_each, blocks)
    cell_term = jnp.einsum(
        "ecmj,cxmpjq->ecxpq", selector, visibility, precision=lax.Precision.HIGHEST
    )
    return lax.psum_scatter(cell_term, "bl", scatter_dimension=0, tiled=True)


def solution(mesh):
    return jax.shard_map(
        shards,
        mesh=mesh,
        in_specs=(P("ct", "bl"), P("ct", None), P("ct", None), P("ct", None)),
        out_specs=P("bl", "ct", None, None, None),
        check_vma=False,
    )
```

profile of v0, /device:TPU:1, one launch (start us, length us, event | category | flops | bytes accessed | tf_op | source)
XLA Modules:
  0.0 138.1 jit_solution(12725136759354073979)
XLA Ops:
  6.5 1.0 copy.82
  7.6 3.9 %collective-permute-start = (bf16[8,3,512]{2,1,0:T(4,128)(2,1)S(1)}, bf16[8,3,512]{2,1,0:T(4,128)(2,1)S(1)}, u32[]{:S(2)}, u32[]{:S(2)}) collective-permute-start(bf16[8,3,512]{2,1,0:T(4,128)(2,1)S(1)} %slice.53), channel_id=1, source_target_pairs={{0,1},{1,2},{2,3},{4,5},{5,6},{6,7},{8,9},{9,10},{10,11},{12,13},{... | collective-permute-start | bytes 73736 | tf_op jit(solution)/shard_map/ppermute | solution.py:18
  11.6 2.1 %sine_negate_fusion = (f32[512,256]{1,0:T(8,128)S(1)}, f32[512,256]{1,0:T(8,128)S(1)}) fusion(), kind=kLoop, calls=%fused_computation.30 | loop fusion | flops 1966080 | bytes 1048576 | tf_op jit(solution)/shard_map/neg | solution.py:33
  13.9 0.4 multiply_convert_fusion
  14.3 0.5 copy-done
  15.2 0.4 copy-done.1
  16.7 1.1 copy.52
  17.8 0.8 reshape.324
  18.6 32.0 %all_to_all.18 = bf16[128,2,512]{2,1,0:T(2,128)(2,1)S(1)} all-to-all(bf16[128,2,512]{2,1,0:T(2,128)(2,1)S(1)} %reshape.324), channel_id=1, replica_groups=mesh['ct'=128,'bl'=4] {'ct'}, dimensions={0} | all-to-all | bytes 524288 | tf_op jit(solution)/shard_map/all_to_all | solution.py:65
  50.6 0.5 reshape.325
  51.3 1.2 copy.55
  53.3 0.6 gather_fusion.1
  54.0 0.6 gather_fusion
  54.8 19.1 %all-gather.2.cloned.1.call-done = bf16[2,2,1024,128]{2,1,0,3:T(2,128)(2,1)} async-done(((bf16[2,2,1024,32]{2,1,0,3:T(2,128)(2,1)}), bf16[2,2,1024,128]{2,1,0,3:T(2,128)(2,1)}) %all-gather.2.cloned.1.call-update) | async-done | bytes 1048592 | tf_op jit(solution)/shard_map/all_gather | solution.py:72
  73.9 1.1 constant_dynamic-slice_fusion
  75.3 2.5 %convolution_bitcast_fusion = f32[2,2,2,256,1024]{3,4,1,2,0:T(8,128)S(1)} fusion(bf16[2,2,1024,128,1]{2,1,0,3,4:T(2,128)(2,1)} %bitcast.68, bf16[2,2,256,128]{3,2,0,1:T(8,128)(2,1)S(1)} %copy.74), kind=kOutput, calls=%fused_computation.7 | convolution fusion | flops 536870912 | bytes 9699328 | tf_op jit(solution)/shard_map/acps,bcqs->cabpq/dot_general | solution.py:76
  77.8 2.5 %slice_add_fusion = (f32[2,1,1,256,1024]{3,4,1,2,0:T(8,128)}, f32[2,1,1,256,1024]{3,4,1,2,0:T(8,128)}) fusion(f32[2,2,2,256,1024]{3,4,1,2,0:T(8,128)S(1)} %convolution_bitcast_fusion), kind=kLoop, calls=%fused_computation.9 | loop fusion | flops 1048576 | bytes 12582912 | tf_op jit(solution)/shard_map/add | solution.py:80
  80.3 2.3 %add.221 = f32[2,1,2,128,8,128]{3,2,5,4,0,1:T(2,128)S(1)} reshape(f32[2,1,1,256,1024]{3,4,1,2,0:T(8,128)} %get-tuple-element.5) | data formatting | bytes 4194304 | tf_op jit(solution)/shard_map/add | solution.py:80
  82.6 2.0 %copy.58 = f32[2,1,2,128,8,128]{5,4,2,3,1,0:T(8,128)} copy(f32[2,1,2,128,8,128]{3,2,5,4,0,1:T(2,128)S(1)} %add.221) | data formatting | bytes 4194304 | tf_op jit(solution)/shard_map/add | solution.py:80
  84.6 2.3 %sub.83 = f32[2,1,2,128,8,128]{3,2,5,4,0,1:T(2,128)S(1)} reshape(f32[2,1,1,256,1024]{3,4,1,2,0:T(8,128)} %get-tuple-element.6) | data formatting | bytes 4194304 | tf_op jit(solution)/shard_map/sub | solution.py:80
  86.9 2.0 %copy.59 = f32[2,1,2,128,8,128]{5,4,2,3,1,0:T(8,128)} copy(f32[2,1,2,128,8,128]{3,2,5,4,0,1:T(2,128)S(1)} %sub.83) | data formatting | bytes 4194304 | tf_op jit(solution)/shard_map/sub | solution.py:80
  89.0 4.0 %fusion.4 = f32[8,2,2,128,128]{4,0,3,2,1:T(8,128)S(1)} fusion(f32[2,1,2,128,8,128]{5,4,2,3,1,0:T(8,128)} %copy.59, f32[2,1,2,128,8,128]{5,4,2,3,1,0:T(8,128)} %copy.58, f32[2,2,8]{2,1,0:T(2,128)S(1)} %select_multiply_fusion, s32[2,2,8]{2,1,0:T(2,128)S(1)} %broadcast_select_fusion.1), kind=kOutput, calls=%fused_computation.10 | convolution fusion | flops 101712384 | bytes 6291712 | tf_op jit(solution)/shard_map/ecmj,cxmpjq->ecxpq/dot_general | solution.py:97
  93.0 1.7 %copy.64 = f32[8,2,2,128,128]{4,3,2,1,0:T(8,128)} copy(f32[8,2,2,128,128]{4,0,3,2,1:T(8,128)S(1)} %fusion.4) | data formatting | bytes 4194304 | tf_op jit(solution)/shard_map/ecmj,cxmpjq->ecxpq/transpose | solution.py:97
  94.7 36.5 %reduce-scatter.2.cloned.1.call-done = f32[2,2,2,128,128]{4,3,2,1,0:T(8,128)} async-done(((f32[8,2,2,128,128]{4,3,2,1,0:T(8,128)}), f32[2,2,2,128,128]{4,3,2,1,0:T(8,128)}) %reduce-scatter.2.cloned.1.call-update) | async-done | bytes 524304 | tf_op jit(solution)/shard_map/reduce_scatter | solution.py:100
  (40 shorter events, 3.2 us)
Async XLA Ops:
  6.5 67.4 %all-gather.2.cloned.1.call-start = ((), (), s32[]{:S(2)}) async-start(), calls=%async_computation.2 | async-start | bytes 1310720 | tf_op jit(solution)/shard_map/all_gather | solution.py:72
  7.6 8.0 %collective-permute-start = (bf16[8,3,512]{2,1,0:T(4,128)(2,1)S(1)}, bf16[8,3,512]{2,1,0:T(4,128)(2,1)S(1)}, u32[]{:S(2)}, u32[]{:S(2)}) collective-permute-start(bf16[8,3,512]{2,1,0:T(4,128)(2,1)S(1)} %slice.53), channel_id=1, source_target_pairs={{0,1},{1,2},{2,3},{4,5},{5,6},{6,7},{8,9},{9,10},{10,11},{12,13},{... | collective-permute-start | bytes 73736 | tf_op jit(solution)/shard_map/ppermute | solution.py:18
  13.9 1.0 copy-start
  14.8 0.7 copy-start.1
  51.1 2.1 %copy-start.2 = (f32[2,36]{1,0:T(2,128)S(1)}, f32[2,36]{1,0:T(2,128)}, u32[]{:S(2)}) copy-start(f32[2,36]{1,0:T(2,128)} %param.7) | copy-start | bytes 868
  51.1 2.8 %copy-start.3 = (s32[2,36]{1,0:T(2,128)S(1)}, s32[2,36]{1,0:T(2,128)}, u32[]{:S(2)}) copy-start(s32[2,36]{1,0:T(2,128)} %param.6) | copy-start | bytes 868
  52.5 78.7 %reduce-scatter.2.cloned.1.call-start = ((), (), s32[]{:S(2)}) async-start(), calls=%async_computation.3 | async-start | bytes 2621440 | tf_op jit(solution)/shard_map/reduce_scatter | solution.py:100
Sparse Core Ops, SparseCore 0:
  52.6 21.2 all-gather.1
  94.9 36.3 reduce-scatter.1
where the time goes:
time: 138 us
  waiting for transfers between devices  55.6 us (40%)
  blocking collectives  32 us (23%)
  local copies, waits for them, and re-layouts  19.5 us (14%)
  between operations  13.6 us (10%)
  matrix products  7.79 us (6%)
  other arithmetic  5.36 us (4%)
  starting transfers between devices  4.17 us (3%)
    reduce_scatter x1, waiting for transfers between devices, shards(): return lax.psum_scatter(cell_term, 'bl', scatter_dimension=0, tiled=True)  36.5 us
    all_to_all x1, blocking collectives, shards(): lax.all_to_all(spectra, 'ct', split_axis=1, concat_axis=2, tiled=True)  32 us
    all_gather x1, waiting for transfers between devices, shards(): shard_part = lax.all_gather(turned, 'bl', axis=3, tiled=True)  19.1 us
    sub x2, local copies, waits for them, and re-layouts, shards(): products[:, 1, 0] - products[:, 0, 1]  4.33 us
    add x2, local copies, waits for them, and re-layouts, shards(): products[:, 0, 0] + products[:, 1, 1]  4.33 us
    dot_general x1, matrix products, shards(): jnp.einsum('ecmj,cxmpjq->ecxpq', selector, visibility, precision=lax.Prec...  4.02 us
    ppermute x1, starting transfers between devices, from_behind(): return lax.ppermute(value, axis, pairs)  3.95 us
    unnamed x13, local copies, waits for them, and re-layouts  3.65 us
  transfers between devices with their start and end apart: 3, of which 2 were waited for; matrix products, arithmetic and copies ran while one was open for 4% of the time, Pallas kernels for 0%

commit v1 on v0

--- a/solution.py
+++ b/solution.py
@@ -69,7 +69,9 @@
     cell_count = CELL_DEV * bl_size
     weights = tile_weight * (1.0 / math.sqrt(SPECTRA))
     rows_each = blocks // bl_size
-    shard_part = lax.all_gather(turned, "bl", axis=3, tiled=True)
+    shard_part = jnp.concatenate(
+        lax.all_to_all(jnp.stack([turned] * lax.axis_size("bl")), "bl", 0, 0), axis=3
+    )
     row_part = lax.dynamic_slice_in_dim(
         shard_part, bl_index * rows_each * BLOCK, rows_each * BLOCK, 2
     )

time: 138 us -> 125 us (0.906)
  blocking collectives: 32 us -> 0 us
  starting transfers between devices: 4.17 us -> 25.6 us
  waiting for transfers between devices: 55.6 us -> 54.2 us
    all_to_all x1 -> x0, blocking collectives: 32 us -> none  [shards(): lax.all_to_all(spectra, 'ct', split_axis=1, concat_axis=2, tiled=True)]
    all_to_all x0 -> x2, waiting for transfers between devices: none -> 25.2 us  [the longest x1 13.8 us: shards(): lax.all_to_all(spectra, 'ct', split_axis=1, concat_axis=2, tiled=True)]
    all_to_all x0 -> x2, starting transfers between devices: none -> 21.6 us  [the longest x1 17.9 us: shards(): lax.all_to_all(spectra, 'ct', split_axis=1, concat_axis=2, tiled=True)]
    all_gather x1 -> x0, waiting for transfers between devices: 19.1 us -> none  [shards(): shard_part = lax.all_gather(turned, 'bl', axis=3, tiled=True)]
    reduce_scatter x1, waiting for transfers between devices: 36.5 us -> 29 us  [shards(): return lax.psum_scatter(cell_term, 'bl', scatter_dimension=0, tiled=True)]
    another operation x0 -> x2, local copies, waits for them, and re-layouts: none -> 1.43 us  [shards(): jnp.stack([turned] * lax.axis_size('bl'))]
  transfers between devices with their start and end apart: 3 -> 4, of which waited for: 2 -> 3; matrix products, arithmetic and copies ran while one was open for 4% -> 4% of each run, Pallas kernels for 0% -> 0%
where the time goes in v1:
time: 125 us
  waiting for transfers between devices  54.2 us (43%)
  starting transfers between devices  25.6 us (20%)
  local copies, waits for them, and re-layouts  19.4 us (16%)
  between operations  13.6 us (11%)
  matrix products  6.56 us (5%)
  other arithmetic  5.35 us (4%)
    reduce_scatter x1, waiting for transfers between devices, shards(): return lax.psum_scatter(cell_term, 'bl', scatter_dimension=0, tiled=True)  29 us
    all_to_all x1, starting transfers between devices, shards(): lax.all_to_all(spectra, 'ct', split_axis=1, concat_axis=2, tiled=True)  17.9 us
    all_to_all x1, waiting for transfers between devices, shards(): lax.all_to_all(spectra, 'ct', split_axis=1, concat_axis=2, tiled=True)  13.8 us
    all_to_all x1, waiting for transfers between devices, shards(): lax.all_to_all(jnp.stack([turned] * lax.axis_size('bl')), 'bl', 0, 0)  11.4 us
    sub x2, local copies, waits for them, and re-layouts, shards(): products[:, 1, 0] - products[:, 0, 1]  4.33 us
    add x2, local copies, waits for them, and re-layouts, shards(): products[:, 0, 0] + products[:, 1, 1]  4.33 us
    unnamed x13, local copies, waits for them, and re-layouts  4.3 us
    dot_general x1, matrix products, shards(): jnp.einsum('ecmj,cxmpjq->ecxpq', selector, visibility, precision=lax.Prec...  4.02 us
  transfers between devices with their start and end apart: 4, of which 3 were waited for; matrix products, arithmetic and copies ran while one was open for 4% of the time, Pallas kernels for 0%

profile of v1, /device:TPU:1, one launch (start us, length us, event | category | flops | bytes accessed | tf_op | source)
XLA Modules:
  0.0 124.8 jit_solution(3029321702172215120)
XLA Ops:
  6.5 1.0 copy.72
  7.6 3.9 %collective-permute-start = (bf16[8,3,512]{2,1,0:T(4,128)(2,1)S(1)}, bf16[8,3,512]{2,1,0:T(4,128)(2,1)S(1)}, u32[]{:S(2)}, u32[]{:S(2)}) collective-permute-start(bf16[8,3,512]{2,1,0:T(4,128)(2,1)S(1)} %slice.53), channel_id=1, source_target_pairs={{0,1},{1,2},{2,3},{4,5},{5,6},{6,7},{8,9},{9,10},{10,11},{12,13},{... | collective-permute-start | bytes 73736 | tf_op jit(solution)/shard_map/ppermute | solution.py:18
  11.6 2.1 %sine_negate_fusion = (f32[512,256]{1,0:T(8,128)S(1)}, f32[512,256]{1,0:T(8,128)S(1)}) fusion(), kind=kLoop, calls=%fused_computation.30 | loop fusion | flops 1966080 | bytes 1048576 | tf_op jit(solution)/shard_map/neg | solution.py:33
  14.3 0.5 copy-done
  15.2 0.4 copy-done.1
  16.7 1.1 copy.41
  17.8 1.5 %reshape.335 = bf16[128,2,512]{2,1,0:T(2,128)(2,1)} reshape(bf16[256,2,8,32]{3,2,1,0:T(8,128)(2,1)S(1)} %bitcast.71) | data formatting | bytes 524288
  19.3 17.9 %all-to-all-start = ((bf16[128,2,512]{2,1,0:T(2,128)(2,1)}), bf16[128,2,512]{2,1,0:T(2,128)(2,1)S(1)}, u32[]{:S(2)}, u32[]{:S(2)}) async-start(bf16[128,2,512]{2,1,0:T(2,128)(2,1)} %reshape.335), calls=%async_computation | async-start | bytes 524288 | tf_op jit(solution)/shard_map/all_to_all | solution.py:65
  37.6 13.8 %all-to-all-done = bf16[128,2,512]{2,1,0:T(2,128)(2,1)S(1)} async-done(((bf16[128,2,512]{2,1,0:T(2,128)(2,1)}), bf16[128,2,512]{2,1,0:T(2,128)(2,1)S(1)}, u32[]{:S(2)}, u32[]{:S(2)}) %all-to-all-start) | async-done | bytes 262176 | tf_op jit(solution)/shard_map/all_to_all | solution.py:65
  51.4 0.5 reshape.336
  52.5 1.1 stack.7
  53.6 3.7 %all-to-all-start.1 = ((bf16[4,2,2,1024,32]{3,4,2,1,0:T(8,128)(2,1)}), bf16[4,2,2,1024,32]{3,4,2,1,0:T(8,128)(2,1)S(1)}, u32[]{:S(2)}, u32[]{:S(2)}) async-start(bf16[4,2,2,1024,32]{3,4,2,1,0:T(8,128)(2,1)} %stack.7), calls=%async_computation.1 | async-start | bytes 2097152 | tf_op jit(solution)/shard_map/all_to_all | solution.py:73
  57.5 0.6 gather_fusion.1
  58.2 0.6 gather_fusion
  59.0 11.4 %all-to-all-done.1 = bf16[4,2,2,1024,32]{3,4,2,1,0:T(8,128)(2,1)S(1)} async-done(((bf16[4,2,2,1024,32]{3,4,2,1,0:T(8,128)(2,1)}), bf16[4,2,2,1024,32]{3,4,2,1,0:T(8,128)(2,1)S(1)}, u32[]{:S(2)}, u32[]{:S(2)}) %all-to-all-start.1) | async-done | bytes 1048608 | tf_op jit(solution)/shard_map/all_to_all | solution.py:73
  70.7 1.3 %convolution_bitcast_fusion = f32[2,2,2,256,1024]{3,4,1,2,0:T(8,128)S(1)} fusion(bf16[2,2,1024,128,1]{2,3,1,0,4:T(8,128)(2,1)S(1)} %bitcast.70, bf16[2,2,256,128]{3,2,0,1:T(8,128)(2,1)S(1)} %copy.64), kind=kOutput, calls=%fused_computation.7 | convolution fusion | flops 536870912 | bytes 9699328 | tf_op jit(solution)/shard_map/acps,bcqs->cabpq/dot_general | solution.py:78
  72.0 2.5 %slice_add_fusion = (f32[2,1,1,256,1024]{3,4,1,2,0:T(8,128)}, f32[2,1,1,256,1024]{3,4,1,2,0:T(8,128)}) fusion(f32[2,2,2,256,1024]{3,4,1,2,0:T(8,128)S(1)} %convolution_bitcast_fusion), kind=kLoop, calls=%fused_computation.9 | loop fusion | flops 1048576 | bytes 12582912 | tf_op jit(solution)/shard_map/add | solution.py:82
  74.5 2.3 %add.221 = f32[2,1,2,128,8,128]{3,2,5,4,0,1:T(2,128)S(1)} reshape(f32[2,1,1,256,1024]{3,4,1,2,0:T(8,128)} %get-tuple-element.5) | data formatting | bytes 4194304 | tf_op jit(solution)/shard_map/add | solution.py:82
  76.8 2.0 %copy.48 = f32[2,1,2,128,8,128]{5,4,2,3,1,0:T(8,128)} copy(f32[2,1,2,128,8,128]{3,2,5,4,0,1:T(2,128)S(1)} %add.221) | data formatting | bytes 4194304 | tf_op jit(solution)/shard_map/add | solution.py:82
  78.8 2.3 %sub.83 = f32[2,1,2,128,8,128]{3,2,5,4,0,1:T(2,128)S(1)} reshape(f32[2,1,1,256,1024]{3,4,1,2,0:T(8,128)} %get-tuple-element.6) | data formatting | bytes 4194304 | tf_op jit(solution)/shard_map/sub | solution.py:82
  81.1 2.0 %copy.49 = f32[2,1,2,128,8,128]{5,4,2,3,1,0:T(8,128)} copy(f32[2,1,2,128,8,128]{3,2,5,4,0,1:T(2,128)S(1)} %sub.83) | data formatting | bytes 4194304 | tf_op jit(solution)/shard_map/sub | solution.py:82
  83.2 4.0 %fusion.4 = f32[8,2,2,128,128]{4,0,3,2,1:T(8,128)S(1)} fusion(f32[2,1,2,128,8,128]{5,4,2,3,1,0:T(8,128)} %copy.49, f32[2,1,2,128,8,128]{5,4,2,3,1,0:T(8,128)} %copy.48, f32[2,2,8]{2,1,0:T(2,128)S(1)} %select_multiply_fusion, s32[2,2,8]{2,1,0:T(2,128)S(1)} %broadcast_select_fusion.1), kind=kOutput, calls=%fused_computation.10 | convolution fusion | flops 101712384 | bytes 6291712 | tf_op jit(solution)/shard_map/ecmj,cxmpjq->ecxpq/dot_general | solution.py:99
  87.2 1.7 %copy.54 = f32[8,2,2,128,128]{4,3,2,1,0:T(8,128)} copy(f32[8,2,2,128,128]{4,0,3,2,1:T(8,128)S(1)} %fusion.4) | data formatting | bytes 4194304 | tf_op jit(solution)/shard_map/ecmj,cxmpjq->ecxpq/transpose | solution.py:99
  88.9 29.0 %reduce-scatter.2.cloned.1.call-done = f32[2,2,2,128,128]{4,3,2,1,0:T(8,128)} async-done(((f32[8,2,2,128,128]{4,3,2,1,0:T(8,128)}), f32[2,2,2,128,128]{4,3,2,1,0:T(8,128)}) %reduce-scatter.2.cloned.1.call-update) | async-done | bytes 524304 | tf_op jit(solution)/shard_map/reduce_scatter | solution.py:102
  (42 shorter events, 3.8 us)
Async XLA Ops:
  7.6 8.0 %collective-permute-start = (bf16[8,3,512]{2,1,0:T(4,128)(2,1)S(1)}, bf16[8,3,512]{2,1,0:T(4,128)(2,1)S(1)}, u32[]{:S(2)}, u32[]{:S(2)}) collective-permute-start(bf16[8,3,512]{2,1,0:T(4,128)(2,1)S(1)} %slice.53), channel_id=1, source_target_pairs={{0,1},{1,2},{2,3},{4,5},{5,6},{6,7},{8,9},{9,10},{10,11},{12,13},{... | collective-permute-start | bytes 73736 | tf_op jit(solution)/shard_map/ppermute | solution.py:18
  13.9 1.0 copy-start
  14.8 0.7 copy-start.1
  16.6 21.0 %copy-start.2 = (f32[2,36]{1,0:T(2,128)S(1)}, f32[2,36]{1,0:T(2,128)}, u32[]{:S(2)}) copy-start(f32[2,36]{1,0:T(2,128)} %param.7) | copy-start | bytes 868
  19.3 32.1 %all-to-all-start = ((bf16[128,2,512]{2,1,0:T(2,128)(2,1)}), bf16[128,2,512]{2,1,0:T(2,128)(2,1)S(1)}, u32[]{:S(2)}, u32[]{:S(2)}) async-start(bf16[128,2,512]{2,1,0:T(2,128)(2,1)} %reshape.335), calls=%async_computation | async-start | bytes 524288 | tf_op jit(solution)/shard_map/all_to_all | solution.py:65
  52.1 6.0 %copy-start.3 = (s32[2,36]{1,0:T(2,128)S(1)}, s32[2,36]{1,0:T(2,128)}, u32[]{:S(2)}) copy-start(s32[2,36]{1,0:T(2,128)} %param.6) | copy-start | bytes 868
  53.6 16.8 %all-to-all-start.1 = ((bf16[4,2,2,1024,32]{3,4,2,1,0:T(8,128)(2,1)}), bf16[4,2,2,1024,32]{3,4,2,1,0:T(8,128)(2,1)S(1)}, u32[]{:S(2)}, u32[]{:S(2)}) async-start(bf16[4,2,2,1024,32]{3,4,2,1,0:T(8,128)(2,1)} %stack.7), calls=%async_computation.1 | async-start | bytes 2097152 | tf_op jit(solution)/shard_map/all_to_all | solution.py:73
  57.3 60.6 %reduce-scatter.2.cloned.1.call-start = ((), (), s32[]{:S(2)}) async-start(), calls=%async_computation.3 | async-start | bytes 2621440 | tf_op jit(solution)/shard_map/reduce_scatter | solution.py:102
Sparse Core Ops, SparseCore 0:
  89.0 28.8 reduce-scatter.1
